TPU v7x, 128 devices: a whole 4x4x4 slice. The times are simulated.
128 devices in a mesh: clus: 16 (over y, x), leaf: 8 (over z, core).
Axes of the slice: x: 4, y: 4, z: 4, core: 2. Of those that a mesh axis runs over, the one named last changes fastest.
Arguments:
- right_sides: bfloat16 [32, 8, 98304], P(None, 'leaf', 'clus'), may hold values from -6 to 6
- near_blocks: bfloat16 [8, 384, 5, 256, 256], P('leaf', 'clus'), may hold values from -0.15625 to 0.15625
- near_cols: int32 [8, 384, 5], P('leaf', 'clus'), may hold values from 0 to 383, as said below
- near_count: int32 [8, 384], P('leaf', 'clus'), may hold values from 1 to 5, as said below
- basis: bfloat16 [8, 384, 256, 64], P('leaf', 'clus'), may hold values from -0.375 to 0.375
- leaf_transfer: bfloat16 [8, 384, 64, 64], P('leaf', 'clus'), may hold values from -0.75 to 0.75
- par_transfer: bfloat16 [8, 96, 64, 64], P('leaf', 'clus'), may hold values from -0.75 to 0.75
- leaf_src: int32 [8, 384, 8], P('leaf', 'clus'), may hold values from 0 to 383, as said below
- leaf_coup: bfloat16 [8, 384, 8, 64, 64], P('leaf', 'clus'), may hold values from -0.25 to 0.25
- par_src: int32 [8, 96, 27], P('leaf', 'clus'), may hold values from 0 to 767, as said below
- par_coup: bfloat16 [8, 96, 27, 64, 64], P('leaf', 'clus'), may hold values from -0.15625 to 0.15625
- top_src: int32 [8, 16, 27], P('leaf', 'clus'), may hold values from 0 to 127
- top_coup: bfloat16 [8, 16, 27, 64, 64], P('leaf', 'clus'), may hold values from -0.15625 to 0.15625
Outputs:
- product: bfloat16 [32, 8, 98304], P(None, 'leaf', 'clus')
Inputs may be any that keep to these rules, and one draw needn't show every extreme that they name: near_cols[s, g, 0] is g; the other slots name leaves within 8 of g in the same subtree. `near_count`: each subtree has a leaf with all 5 slots used. `leaf_src`: each entry names a leaf other than g within 8 of g in the same subtree. `par_src`: parent q is parent q % 96 of subtree q // 96; among the 162 entries of the parents of one device, at most 3 name parents held by one device, and some device is named exactly 3 times.
All inputs are finite; a program needn't handle non-finite values.
Results may differ from a plain program's by a relative error of at most 0.015.
Values may be sent and summed in bfloat16 or wider, within the bound.
A program may use at most 128 MiB of HBM per device.

v0:
```python
import jax
import jax.numpy as jnp
from jax import lax
from jax.sharding import PartitionSpec as P

REACH = 8


def extended_2(x, sides, width):
    for axis, dim in sides:
        size, length = (lax.axis_size(axis), x.shape[dim])
        up = [(i, (i + 1) % size) for i in range(size - 1)]
        down = [(j, i) for i, j in up]
        last = lax.slice_in_dim(x, length - width, length, axis=dim)
        first = lax.slice_in_dim(x, 0, width, axis=dim)
        before = lax.ppermute(last, axis, up)
        after = lax.ppermute(first, axis, down)
        x = jnp.concatenate([before, x, after], axis=dim)
    return x


def local(
    right_sides,
    near_blocks,
    near_cols,
    near_count,
    basis,
    leaf_transfer,
    par_transfer,
    leaf_src,
    leaf_coup,
    par_src,
    par_coup,
    top_src,
    top_coup,
):
    vectors = right_sides.shape[0]
    leaf_count = basis.shape[1]
    leaf_size = basis.shape[2]
    basis_rank = basis.shape[3]
    parent_count = par_transfer.shape[1]
    cluster_count = lax.axis_size("clus")
    subtree_count = lax.axis_size("leaf")
    tile_size = vectors * basis_rank
    offset = lax.axis_index("clus") * leaf_count - REACH
    extended = extended_2(right_sides, (("clus", 2),), REACH * leaf_size)
    leaves = right_sides.reshape(vectors, leaf_count, leaf_size)
    leaf_coeff = jnp.einsum(
        "rlb,lbk->lrk", leaves, basis[0], preferred_element_type=jnp.float32
    ).astype(jnp.bfloat16)
    parent_coeff = jnp.einsum(
        "pcrk,pckm->prm",
        leaf_coeff.reshape(parent_count, 4, vectors, basis_rank),
        leaf_transfer[0].reshape(parent_count, 4, basis_rank, basis_rank),
        preferred_element_type=jnp.float32,
    ).astype(jnp.bfloat16)
    top_coeff = jnp.einsum(
        "prk,pkm->rm", parent_coeff, par_transfer[0], preferred_element_type=jnp.float32
    ).astype(jnp.bfloat16)
    top_sources = top_src[0, 0]
    joined_tops = top_sources % cluster_count * subtree_count + top_sources // cluster_count
    top_blocks = top_coup[0, 0]
    piece = lax.all_gather(top_coeff.reshape(1, tile_size), ("clus", "leaf"), axis=0, tiled=True)
    numbers = lax.broadcasted_iota(jnp.int32, (1, piece.shape[0]), 1)
    select = (joined_tops[:, None] == numbers).astype(jnp.bfloat16)
    coeffs = jnp.dot(select, piece, preferred_element_type=jnp.float32).astype(jnp.bfloat16)
    coeffs = coeffs.reshape(-1, vectors, basis_rank)
    top_field = jnp.einsum(
        "jrk,jkm->rm", coeffs, top_blocks, preferred_element_type=jnp.float32
    ).astype(jnp.bfloat16)
    flat_parent = parent_coeff.reshape(parent_count, tile_size)
    wanted = par_src[0].reshape(-1)
    per_tree = cluster_count * parent_count
    source_tree = wanted // per_tree
    within_tree = wanted % per_tree
    source_clus = within_tree // parent_count
    source_local = within_tree % parent_count
    source_device = source_clus * subtree_count + source_tree
    every_parent = lax.all_gather(flat_parent, ("clus", "leaf"), axis=0, tiled=True)
    fetched = jnp.take(every_parent, source_device * parent_count + source_local, axis=0)
    fetched = fetched.reshape(parent_count, -1, vectors, basis_rank)
    par_field = jnp.einsum(
        "pjrk,pjkm->prm", fetched, par_coup[0], preferred_element_type=jnp.float32
    )
    par_field = par_field + jnp.einsum(
        "rm,pkm->prk", top_field, par_transfer[0], preferred_element_type=jnp.float32
    )
    par_field = par_field.astype(jnp.bfloat16)
    leaf_rim = extended_2(leaf_coeff.reshape(leaf_count, tile_size), (("clus", 0),), REACH)
    leaf_rim = leaf_rim.reshape(leaf_count + 2 * REACH, vectors, basis_rank)
    partners = jnp.take(leaf_rim, leaf_src[0] - offset, axis=0)
    leaf_field = jnp.einsum(
        "ljrk,ljkm->lrm", partners, leaf_coup[0], preferred_element_type=jnp.float32
    )
    parent_down = jnp.repeat(par_field, 4, axis=0)
    leaf_field = leaf_field + jnp.einsum(
        "lrm,lkm->lrk", parent_down, leaf_transfer[0], preferred_element_type=jnp.float32
    )
    leaf_field = leaf_field.astype(jnp.bfloat16)
    extended = extended.reshape(vectors, leaf_count + 2 * REACH, leaf_size)
    picked = jnp.take(extended, near_cols[0] - offset, axis=1)
    slot_ids_near = lax.broadcasted_iota(jnp.int32, (leaf_count, near_cols.shape[2]), 1)
    live_mask = (slot_ids_near < near_count[0][:, None]).astype(jnp.bfloat16)
    picked = picked * live_mask[None, :, :, None]
    near_sum = jnp.einsum(
        "rlnb,lnbc->rlc", picked, near_blocks[0], preferred_element_type=jnp.float32
    )
    far_sum = jnp.einsum("lrk,lbk->rlb", leaf_field, basis[0], preferred_element_type=jnp.float32)
    return (near_sum + far_sum).reshape(vectors, 1, leaf_count * leaf_size).astype(jnp.bfloat16)


def solution(mesh):
    return jax.shard_map(
        local,
        mesh=mesh,
        in_specs=(
            P(None, "leaf", "clus"),
            P("leaf", "clus", None, None, None),
            P("leaf", "clus", None),
            P("leaf", "clus"),
            P("leaf", "clus", None, None),
            P("leaf", "clus", None, None),
            P("leaf", "clus", None, None),
            P("leaf", "clus", None),
            P("leaf", "clus", None, None, None),
            P("leaf", "clus", None),
            P("leaf", "clus", None, None, None),
            P("leaf", "clus", None),
            P("leaf", "clus", None, None, None),
        ),
        out_specs=P(None, "leaf", "clus"),
        check_vma=False,
    )
```

profile of v0, /device:TPU:1, one launch (start us, length us, event | category | flops | bytes accessed | tf_op | source)
XLA Modules:
  0.0 137.1 jit_solution(10466139904677206956)
XLA Ops:
  6.6 1.2 copy.64
  7.8 1.5 %convolution_convert_fusion.1 = bf16[24,32,64]{2,1,0:T(8,128)(2,1)S(1)} fusion(bf16[1,24,256,64]{2,3,1,0:T(8,128)(2,1)} %param.17, bf16[32,24,256]{2,1,0:T(8,128)(2,1)S(1)} %bitcast.157), kind=kOutput, calls=%fused_computation.24 | convolution fusion | flops 25214976 | bytes 1277952 | tf_op jit(solution)/shard_map/rlb,lbk->lrk/dot_general | solution.py:48
  10.6 1.6 %slice.21 = bf16[8,2048]{1,0:T(8,128)(2,1)} reshape(bf16[8,32,64]{2,1,0:T(8,128)(2,1)} %get-tuple-element.9) | data formatting | bytes 65536 | tf_op jit(solution)/shard_map/slice | solution.py:14
  12.2 4.5 %collective-permute-start.2 = (bf16[8,2048]{1,0:T(8,128)(2,1)}, bf16[8,2048]{1,0:T(8,128)(2,1)}, u32[]{:S(2)}, u32[]{:S(2)}) collective-permute-start(bf16[8,2048]{1,0:T(8,128)(2,1)} %slice.21), channel_id=1, source_target_pairs={{0,8},{8,16},{16,24},{24,32},{32,40},{40,48},{48,56},{56,64},{64,7... | collective-permute-start | bytes 98312 | tf_op jit(solution)/shard_map/ppermute | solution.py:16
  16.7 1.6 %slice.23 = bf16[8,2048]{1,0:T(8,128)(2,1)} reshape(bf16[8,32,64]{2,1,0:T(8,128)(2,1)} %get-tuple-element.10) | data formatting | bytes 65536 | tf_op jit(solution)/shard_map/slice | solution.py:15
  18.3 1.3 collective-permute-start.3
  19.6 2.0 %fusion.33 = bf16[6,32,64]{2,1,0:T(8,128)(2,1)} fusion(bf16[6,4,32,64]{3,2,1,0:T(8,128)(2,1)} %bitcast.153, bf16[6,4,64,64]{3,2,1,0:T(8,128)(2,1)} %bitcast.158), kind=kOutput, calls=%fused_computation.30 | convolution fusion | flops 6303744 | bytes 319488 | tf_op jit(solution)/shard_map/pcrk,pckm->prm/dot_general | solution.py:51
  21.6 1.5 %reshape.344 = bf16[1,6,2048]{2,1,0:T(8,128)(2,1)} reshape(bf16[6,32,64]{2,1,0:T(8,128)(2,1)} %fusion.33) | data formatting | bytes 49152
  23.8 4.6 %collective-permute-start = (bf16[32,1,2048]{2,0,1:T(8,128)(2,1)}, bf16[32,1,2048]{2,0,1:T(8,128)(2,1)}, u32[]{:S(2)}, u32[]{:S(2)}) collective-permute-start(bf16[32,1,2048]{2,0,1:T(8,128)(2,1)} %get-tuple-element.7), channel_id=1, source_target_pairs={{0,8},{8,16},{16,24},{24,32},{32,40},{40,48},{48,56},{56,64},{64,7... | collective-permute-start | bytes 393224 | tf_op jit(solution)/shard_map/ppermute | solution.py:16
  28.4 1.3 collective-permute-start.1
  33.6 43.4 %all-gather.1 = bf16[128,1,2048]{2,1,0:T(2,128)(2,1)S(1)} all-gather(bf16[1,1,2048]{2,1,0:T(2,128)(2,1)S(1)} %reshape.346), channel_id=1, replica_groups=mesh['clus'=16,'leaf'=8] {'clus','leaf'}, dimensions={0}, use_global_device_ids=true | all-gather | bytes 528384 | tf_op jit(solution)/shard_map/all_gather | solution.py:63
  80.6 1.5 %concatenate.13 = bf16[8,32,64]{2,1,0:T(8,128)(2,1)} reshape(bf16[8,2048]{1,0:T(8,128)(2,1)} %collective-permute-done.3) | data formatting | bytes 65536 | tf_op jit(solution)/shard_map/concatenate | solution.py:18
  83.2 2.1 %gather_fusion.1 = bf16[192,32,64]{2,1,0:T(8,128)(2,1)} fusion(bf16[40,32,64]{2,1,0:T(8,128)(2,1)S(1)} %pad_maximum_fusion.1, s32[1024]{0:T(1024)S(1)} %pad_clamp_fusion.1), kind=kCustom, calls=%fused_computation.1 | custom fusion | bytes 1573632 | tf_op jit(solution)/shard_map/jit(_take)/gather | solution.py:91
  85.2 3.2 %fusion.21 = f32[24,32,64]{2,1,0:T(8,128)} fusion(bf16[1,24,8,64,64]{4,3,2,1,0:T(8,128)(2,1)S(1)} %copy-done, bf16[24,8,32,64]{3,2,1,0:T(8,128)(2,1)} %bitcast.156, pred[24,8]{1,0:T(8,128)(4,1)} %copy.50), kind=kOutput, calls=%fused_computation.22 | convolution fusion | flops 50724864 | bytes 2556096 | tf_op jit(solution)/shard_map/ljrk,ljkm->lrm/dot_general | solution.py:92
  90.6 3.1 %gather_fusion = bf16[120,32,256]{2,1,0:T(8,128)(2,1)} fusion(bf16[32,40,256]{2,0,1:T(8,128)(2,1)} %copy.49, s32[1024]{0:T(1024)S(1)} %pad_clamp_fusion.2), kind=kCustom, calls=%fused_computation | custom fusion | bytes 3932640 | tf_op jit(solution)/shard_map/jit(_take)/gather | solution.py:101
  93.7 9.7 %fusion.14 = f32[24,32,256]{2,1,0:T(8,128)} fusion(bf16[1,24,5,256,256]{4,3,2,1,0:T(8,128)(2,1)} %param.14, bf16[24,5,32,256]{3,2,1,0:T(8,128)(2,1)} %bitcast.151, pred[24,5]{1,0:T(8,128)(4,1)S(1)} %copy-done.5, bf16[24,5]{1,0:T(8,128)(2,1)S(1)} %fusion.53), kind=kOutput, calls=%fused_computation.18 | convolution fusion | flops 505282560 | bytes 18481512 | tf_op jit(solution)/shard_map/rlnb,lnbc->rlc/dot_general | solution.py:105
  103.4 6.3 %reshape.345 = bf16[768,2048]{1,0:T(8,128)(2,1)} reshape(bf16[128,6,2048]{2,1,0:T(8,128)(2,1)} %all-gather.4.cloned.1.call-done) | data formatting | bytes 6291456
  109.8 5.0 %gather_fusion.2 = bf16[162,2048]{1,0:T(8,128)(2,1)} fusion(bf16[768,2048]{1,0:T(8,128)(2,1)} %reshape.345, s32[1024]{0:T(1024)} %pad_clamp_fusion), kind=kCustom, calls=%fused_computation.2 | custom fusion | bytes 1327752 | tf_op jit(solution)/shard_map/jit(_take)/gather | solution.py:80
  114.7 3.1 %gather.17 = bf16[6,27,32,64]{3,2,1,0:T(8,128)(2,1)} reshape(bf16[162,2048]{1,0:T(8,128)(2,1)} %gather_fusion.2) | data formatting | bytes 1327104 | tf_op jit(solution)/shard_map/jit(_take)/gather | solution.py:80
  117.9 3.7 %fusion.27 = f32[6,32,64]{2,1,0:T(8,128)} fusion(bf16[1,6,27,64,64]{4,3,2,1,0:T(8,128)(2,1)} %param.23, bf16[6,27,32,64]{3,2,1,0:T(8,128)(2,1)} %gather.17, pred[6,27]{1,0:T(8,128)(4,1)S(1)} %copy-done.9), kind=kOutput, calls=%fused_computation.26 | convolution fusion | flops 42799104 | bytes 2039970 | tf_op jit(solution)/shard_map/pjrk,pjkm->prm/dot_general | solution.py:82
  121.6 2.2 %fusion.34 = bf16[6,32,64]{2,1,0:T(8,128)(2,1)} fusion(f32[6,32,64]{2,1,0:T(8,128)} %fusion.27, bf16[27,32,64]{2,1,0:T(8,128)(2,1)} %reshape.316, bf16[1,1,27,64,64]{4,3,2,1,0:T(8,128)(2,1)} %param.25, bf16[1,6,64,64]{3,2,1,0:T(8,128)(2,1)} %param.19), kind=kOutput, calls=%fused_computation.31 | convolution fusion | flops 8677376 | bytes 454656 | tf_op jit(solution)/shard_map/rm,pkm->prk/dot_general | solution.py:85
  123.8 1.5 %broadcast_in_dim.41 = bf16[6,4,32,64]{3,2,1,0:T(8,128)(2,1)} broadcast(bf16[6,32,64]{2,1,0:T(8,128)(2,1)} %fusion.34), dimensions={0,2,3} | broadcast | bytes 122880 | tf_op jit(solution)/shard_map/broadcast_in_dim | solution.py:95
  125.3 2.8 %fusion.20 = bf16[32,24,256]{2,0,1:T(8,128)(2,1)} fusion(f32[24,32,256]{2,1,0:T(8,128)} %fusion.14, f32[24,32,64]{2,1,0:T(8,128)} %fusion.21, bf16[24,32,64]{2,1,0:T(8,128)(2,1)} %bitcast.159, bf16[1,24,256,64]{2,3,1,0:T(8,128)(2,1)} %param.17, bf16[1,24,64,64]{3,2,1,0:T(8,128)(2,1)S(1)} %copy-done.4), kind=kOutput, calls=%fused_computation.21 | convolution fusion | flops 31948800 | bytes 2457600 | tf_op jit(solution)/shard_map/lrk,lbk->rlb/dot_general | solution.py:108
  128.1 1.2 copy.56
  (64 shorter events, 13.6 us)
Async XLA Ops:
  6.5 78.7 %copy-start = (bf16[1,24,8,64,64]{4,3,2,1,0:T(8,128)(2,1)S(1)}, bf16[1,24,8,64,64]{4,3,2,1,0:T(8,128)(2,1)}, u32[]{:S(2)}) copy-start(bf16[1,24,8,64,64]{4,3,2,1,0:T(8,128)(2,1)} %param.21) | copy-start | bytes 4718596
  6.5 16.6 %copy-start.1 = (bf16[32,1,6144]{2,0,1:T(8,128)(2,1)S(1)}, bf16[32,1,6144]{2,0,1:T(8,128)(2,1)}, u32[]{:S(2)}) copy-start(bf16[32,1,6144]{2,0,1:T(8,128)(2,1)} %param.13) | copy-start | bytes 1179652
  6.5 23.2 %copy-start.7 = (s32[1,24,8]{1,2,0:T(8,128)S(1)}, s32[1,24,8]{1,2,0:T(8,128)}, u32[]{:S(2)}) copy-start(s32[1,24,8]{1,2,0:T(8,128)} %param.20) | copy-start | bytes 2308
  6.5 96.9 %all-gather.4.cloned.1.call-start = ((), (), s32[]{:S(2)}) async-start(), calls=%async_computation | async-start | bytes 4227072 | tf_op jit(solution)/shard_map/all_gather | solution.py:79
  6.5 23.4 %copy-start.6 = (s32[1,6,27]{2,0,1:T(1,128)S(1)}, s32[1,6,27]{2,0,1:T(1,128)}, u32[]{:S(2)}) copy-start(s32[1,6,27]{2,0,1:T(1,128)} %param.22) | copy-start | bytes 1948
  6.6 25.4 %copy-start.8 = (s32[1,24,5]{1,0,2:T(1,128)S(1)}, s32[1,24,5]{1,0,2:T(1,128)}, u32[]{:S(2)}) copy-start(s32[1,24,5]{1,0,2:T(1,128)} %param.15) | copy-start | bytes 1444
  6.6 26.3 %copy-start.10 = (s32[1,1,27]{2,1,0:T(1,128)S(1)}, s32[1,1,27]{2,1,0:T(1,128)}, u32[]{:S(2)}) copy-start(s32[1,1,27]{2,1,0:T(1,128)} %param.24) | copy-start | bytes 328
  9.3 0.7 copy-start.3
  12.2 67.5 %collective-permute-start.2 = (bf16[8,2048]{1,0:T(8,128)(2,1)}, bf16[8,2048]{1,0:T(8,128)(2,1)}, u32[]{:S(2)}, u32[]{:S(2)}) collective-permute-start(bf16[8,2048]{1,0:T(8,128)(2,1)} %slice.21), channel_id=1, source_target_pairs={{0,8},{8,16},{16,24},{24,32},{32,40},{40,48},{48,56},{56,64},{64,7... | collective-permute-start | bytes 98312 | tf_op jit(solution)/shard_map/ppermute | solution.py:16
  18.3 62.3 %collective-permute-start.3 = (bf16[8,2048]{1,0:T(8,128)(2,1)}, bf16[8,2048]{1,0:T(8,128)(2,1)}, u32[]{:S(2)}, u32[]{:S(2)}) collective-permute-start(bf16[8,2048]{1,0:T(8,128)(2,1)} %slice.23), channel_id=1, source_target_pairs={{8,0},{16,8},{24,16},{32,24},{40,32},{48,40},{56,48},{64,56},{72,6... | collective-permute-start | bytes 98312 | tf_op jit(solution)/shard_map/ppermute | solution.py:17
  23.8 64.6 %collective-permute-start = (bf16[32,1,2048]{2,0,1:T(8,128)(2,1)}, bf16[32,1,2048]{2,0,1:T(8,128)(2,1)}, u32[]{:S(2)}, u32[]{:S(2)}) collective-permute-start(bf16[32,1,2048]{2,0,1:T(8,128)(2,1)} %get-tuple-element.7), channel_id=1, source_target_pairs={{0,8},{8,16},{16,24},{24,32},{32,40},{40,48},{48,56},{56,64},{64,7... | collective-permute-start | bytes 393224 | tf_op jit(solution)/shard_map/ppermute | solution.py:16
  28.4 60.0 %collective-permute-start.1 = (bf16[32,1,2048]{2,0,1:T(8,128)(2,1)}, bf16[32,1,2048]{2,0,1:T(8,128)(2,1)}, u32[]{:S(2)}, u32[]{:S(2)}) collective-permute-start(bf16[32,1,2048]{2,0,1:T(8,128)(2,1)} %get-tuple-element.8), channel_id=1, source_target_pairs={{8,0},{16,8},{24,16},{32,24},{40,32},{48,40},{56,48},{64,56},{72,6... | collective-permute-start | bytes 393224 | tf_op jit(solution)/shard_map/ppermute | solution.py:17
  85.2 3.2 %copy-start.2 = (bf16[32,1,6144]{2,0,1:T(8,128)(2,1)S(1)}, bf16[32,1,6144]{2,0,1:T(8,128)(2,1)}, u32[]{:S(2)}) copy-start(bf16[32,1,6144]{2,0,1:T(8,128)(2,1)} %param.13) | copy-start | bytes 1179652
  90.6 3.1 %copy-start.5 = (pred[24,5]{1,0:T(8,128)(4,1)S(1)}, pred[24,5]{1,0:T(8,128)(4,1)}, u32[]{:S(2)}) copy-start(pred[24,5]{1,0:T(8,128)(4,1)} %copy.47) | copy-start | bytes 364
  114.7 3.2 %copy-start.9 = (pred[6,27]{1,0:T(8,128)(4,1)S(1)}, pred[6,27]{1,0:T(8,128)(4,1)}, u32[]{:S(2)}) copy-start(pred[6,27]{1,0:T(8,128)(4,1)} %get-tuple-element.5) | copy-start | bytes 490
  117.9 7.4 %copy-start.4 = (bf16[1,24,64,64]{3,2,1,0:T(8,128)(2,1)S(1)}, bf16[1,24,64,64]{3,2,1,0:T(8,128)(2,1)}, u32[]{:S(2)}) copy-start(bf16[1,24,64,64]{3,2,1,0:T(8,128)(2,1)} %param.18) | copy-start | bytes 589828
Sparse Core Ops, SparseCore 0:
  23.2 70.6 all-gather.3
where the time goes:
time: 138 us; the launch traced here: 137 us
  blocking collectives  43.4 us (31%)
  local copies, waits for them, and re-layouts  37.7 us (27%)
  matrix products  26.6 us (19%)
  between operations  13.6 us (10%)
  starting transfers between devices  11.7 us (8%)
  other arithmetic  4.07 us (3%)
    all_gather x1, blocking collectives, local(): lax.all_gather(top_coeff.reshape(1, tile_size), ('clus', 'leaf'), axis=0,...  43.4 us
    unnamed x27, local copies, waits for them, and re-layouts  9.98 us
    dot_general x1, matrix products, local(): jnp.einsum('rlnb,lnbc->rlc', picked, near_blocks[0], preferred_element_ty...  9.73 us
    ppermute x2, starting transfers between devices, extended_2(): before = lax.ppermute(last, axis, up)  9.17 us
    gather x2, local copies, waits for them, and re-layouts, local(): jnp.take(every_parent, source_device * parent_count + source_local, axis=0)  8.12 us
    dot_general x1, matrix products, local(): jnp.einsum('pjrk,pjkm->prm', fetched, par_coup[0], preferred_element_type...  3.72 us
    dot_general x1, matrix products, local(): jnp.einsum('ljrk,ljkm->lrm', partners, leaf_coup[0], preferred_element_ty...  3.19 us
    gather x1, local copies, waits for them, and re-layouts, local(): picked = jnp.take(extended, near_cols[0] - offset, axis=1)  3.13 us
  transfers between devices with their start and end apart: 5, of which 0 were waited for; matrix products, arithmetic and copies ran while one was open for 26% of the time, Pallas kernels for 0%

commit v1 on v0

v1 whole, which is shorter than its diff:
```python
import jax
import jax.numpy as jnp
from jax import lax
from jax.experimental import pallas as pl
from jax.experimental.pallas import tpu as pltpu
from jax.sharding import PartitionSpec as P

F32 = jnp.float32
BF16 = jnp.bfloat16
LEAVES = 24
PARENTS = 6
HALO = 8
NEAR = 5
PTS = 256
ZERO = LEAVES + 2 * HALO
PARTS = (((0, 2), "xyz"), ((2, 2), "yzx"), ((4, 2), "zxy"), (None, "xyz"))


def dot(a, b):
    return lax.dot_general(a, b, (((1,), (0,)), ((), ())), preferred_element_type=F32)


def dot_t(a, b):
    return lax.dot_general(a, b, (((1,), (1,)), ((), ())), preferred_element_type=F32)


def pack(y):
    return jnp.concatenate([y[:16], y[16:]], axis=1).astype(BF16)


def side_by_side(tiles):
    low = lax.broadcasted_iota(jnp.int32, (16, 128), 1) < 64
    columns = []
    for i in range(0, len(tiles), 2):
        a = tiles[i].astype(F32)
        b = tiles[i + 1].astype(F32) if i + 1 < len(tiles) else jnp.zeros_like(a)
        top = jnp.where(low, a, pltpu.roll(b, 64, 1))
        bottom = jnp.where(low, pltpu.roll(a, 64, 1), b)
        columns.append(jnp.concatenate([top, bottom], axis=0).astype(BF16))
    return jnp.concatenate(columns, axis=1)


def kernel(
    rhs, near, cols, count, basis, lt, pt, leaf_src, leaf_coup, par_src, par_coup, top_src, top_coup,
    out,
    x_v, near_v, basis_v, lt_v, pt_v, leaf_coup_v, par_coup_v, top_coup_v, out_v,
    cols_s, count_s, leaf_src_s, par_src_s, top_src_s,
    leaf_t, par_t, top_t, near_acc, leaf_acc,
    x_sem, in_sem, near_sem, halo_send, halo_recv, ag_send, ag_recv, core_send, core_recv, out_sem,
):
    clus = lax.axis_index("clus")
    tree = lax.axis_index("leaf")
    y, x = lax.div(clus, 4), lax.rem(clus, 4)
    z, core = lax.div(tree, 2), lax.rem(tree, 2)

    def device(dz=0, dc=0, dy=0, dx=0):
        return (
            lax.rem(y + dy, 4) * 4 + lax.rem(x + dx, 4),
            lax.rem(z + dz, 4) * 2 + lax.rem(core + dc, 2),
        )

    right, left = (lax.rem(clus + 1, 16), tree), (lax.rem(clus + 15, 16), tree)
    sibling = device(dc=1)
    along = {
        "z": [device(dz=d) for d in (1, 2, 3)],
        "y": [device(dy=d) for d in (1, 2, 3)],
        "x": [device(dx=d) for d in (1, 2, 3)],
    }
    partners = [right, left, sibling] + along["z"] + along["y"] + along["x"]
    barrier = pltpu.get_barrier_semaphore()
    for partner in partners:
        pl.semaphore_signal(barrier, inc=1, device_id=partner, device_id_type=pl.DeviceIdType.MESH)

    def fetch(i, src, dst):
        return pltpu.make_async_copy(src, dst, in_sem.at[i])

    def x_fetch(g):
        return pltpu.make_async_copy(rhs.at[:, pl.ds(g * PTS, PTS)], x_v.at[HALO + g], x_sem.at[g])

    for g in range(LEAVES):
        x_fetch(g).start()
    fetches = [
        fetch(1, basis, basis_v),
        fetch(2, lt, lt_v),
        fetch(3, pt, pt_v),
        fetch(4, cols, cols_s),
        fetch(5, count, count_s),
        fetch(6, leaf_src, leaf_src_s),
        fetch(7, par_src, par_src_s),
        fetch(8, top_src, top_src_s),
        fetch(9, leaf_coup, leaf_coup_v),
        fetch(10, par_coup, par_coup_v),
        fetch(11, top_coup, top_coup_v),
    ]
    for f in fetches[:3]:
        f.start()

    def near_fetch(g):
        return pltpu.make_async_copy(near.at[g], near_v.at[g], near_sem.at[g])

    @pl.loop(0, LEAVES)
    def _(g):
        near_fetch(g).start()

    for f in fetches[3:]:
        f.start()

    def remote(src, dst, send, recv, to):
        return pltpu.make_async_remote_copy(
            src_ref=src, dst_ref=dst, send_sem=send, recv_sem=recv, device_id=to,
            device_id_type=pl.DeviceIdType.MESH,
        )

    x_v[ZERO] = jnp.zeros((32, PTS), BF16)
    pl.semaphore_wait(barrier, len(partners))
    halos = [
        remote(x_v.at[pl.ds(LEAVES, HALO)], x_v.at[pl.ds(0, HALO)], halo_send.at[0], halo_recv.at[0], right),
        remote(x_v.at[pl.ds(HALO, HALO)], x_v.at[pl.ds(LEAVES + HALO, HALO)], halo_send.at[1], halo_recv.at[1], left),
        remote(leaf_t.at[pl.ds(LEAVES, HALO)], leaf_t.at[pl.ds(0, HALO)], halo_send.at[2], halo_recv.at[2], right),
        remote(leaf_t.at[pl.ds(HALO, HALO)], leaf_t.at[pl.ds(LEAVES + HALO, HALO)], halo_send.at[3], halo_recv.at[3], left),
    ]
    for g in range(LEAVES):
        x_fetch(g).wait()
    halos[0].start()
    halos[1].start()
    for f in fetches[:2]:
        f.wait()

    for g in range(LEAVES):
        leaf_t[HALO + g] = pack(dot_t(x_v[HALO + g], basis_v[g]))
    halos[2].start()
    halos[3].start()
    own = par_t.at[z, core, y, x]
    parent_tiles = []
    for p in range(PARENTS):
        lhs = side_by_side([leaf_t[HALO + 4 * p + c] for c in range(4)])
        tile = pack(dot(lhs, lt_v[4 * p:4 * p + 4].reshape(256, 64)))
        parent_tiles.append(tile)
        own[p] = tile
    fetches[2].wait()
    lhs = side_by_side(parent_tiles)
    top_t[z, core, y, x] = pack(dot(lhs, pt_v[...].reshape(PARENTS * 64, 64)))

    def block(part, done):
        rows = PARTS[part][0]
        at = tuple(
            slice(None) if name in done else value
            for name, value in (("z", z), ("core", core), ("y", y), ("x", x))
        )
        if rows is None:
            return top_t.at[at]
        return par_t.at[at + (pl.ds(rows[0], rows[1]),)]

    def hop(part, stage, k):
        order = PARTS[part][1]
        ref = block(part, order[:stage])
        i = (part * 3 + stage) * 3 + k
        return remote(ref, ref, ag_send.at[i], ag_recv.at[i], along[order[stage]][k])

    def stage_start(stage):
        for part in (3, 0, 1, 2):
            for k in range(3):
                hop(part, stage, k).start()

    def stage_wait(stage):
        for part in (3, 0, 1, 2):
            for k in range(3):
                hop(part, stage, k).wait_recv()

    stage_start(0)

    first = clus * LEAVES - HALO

    def near_leaf(g):
        near_fetch(g).wait()
        total = None
        for n in range(NEAR):
            live = jnp.clip(count_s[0, g] - n, 0, 1)
            at = ZERO + live * (jnp.clip(cols_s[n, 0, g] - first, 0, ZERO - 1) - ZERO)
            term = dot(x_v[at], near_v[g, n])
            total = term if total is None else total + term
        near_acc[g] = total

    for f in fetches[3:8]:
        f.wait()
    halos[0].wait()
    halos[1].wait()

    def near_range(lo, hi):
        @pl.loop(lo, hi)
        def _(g):
            near_leaf(g)

    near_range(0, 4)
    stage_wait(0)
    stage_start(1)
    near_range(4, 9)
    stage_wait(1)
    stage_start(2)

    def plane_relay(part):
        ref = block(part, PARTS[part][1][:2])
        return remote(ref, ref, core_send.at[part * 4], core_recv.at[part * 4], sibling)

    def last_relay(part, k):
        axis = PARTS[part][1][2]
        here = {"z": z, "y": y, "x": x}
        here[axis] = lax.rem(here[axis] + 3 - k, 4)
        done = PARTS[part][1][:2]
        at = tuple(
            slice(None) if name in done else value
            for name, value in (("z", here["z"]), ("core", core), ("y", here["y"]), ("x", here["x"]))
        )
        rows = PARTS[part][0]
        ref = top_t.at[at] if rows is None else par_t.at[at + (pl.ds(rows[0], rows[1]),)]
        i = part * 4 + 1 + k
        return remote(ref, ref, core_send.at[i], core_recv.at[i], sibling)

    for part in (3, 0, 1, 2):
        plane_relay(part).start()

    near_range(9, 24)

    halos[2].wait()
    halos[3].wait()
    fetches[8].wait()

    @pl.loop(0, PARENTS)
    def _(p):
        fields = []
        for c in range(4):
            g = 4 * p + c
            total = None
            for half in range(2):
                tiles = []
                for j in range(4 * half, 4 * half + 4):
                    tiles.append(leaf_t[jnp.clip(leaf_src_s[j, g] - first, 0, ZERO - 1)])
                term = dot(side_by_side(tiles), leaf_coup_v[g, 4 * half:4 * half + 4].reshape(256, 64))
                total = term if total is None else total + term
            fields.append(total)
        leaf_acc[p] = jnp.concatenate(fields, axis=1)

    for k in (0, 2, 1):
        for part in (3, 0, 1, 2):
            hop(part, 2, k).wait_recv()
            last_relay(part, k).start()
    for part in (3, 0, 1, 2):
        plane_relay(part).wait_recv()
        for k in (0, 2, 1):
            last_relay(part, k).wait_recv()

    fetches[10].wait()
    total = None
    for j in range(0, 27, 4):
        tiles = []
        for i in range(j, min(j + 4, 27)):
            t = top_src_s[0, 0, i]
            tiles.append(top_t[t >> 5, (t >> 4) & 1, (t >> 2) & 3, t & 3])
        weights = top_coup_v[j:j + len(tiles)].reshape(len(tiles) * 64, 64)
        term = dot(side_by_side(tiles)[:, :len(tiles) * 64], weights)
        total = term if total is None else total + term
    top_field = total.astype(BF16)
    top_down = dot_t(top_field, pt_v[...].reshape(PARENTS * 64, 64))
    fetches[9].wait()
    lane = lax.broadcasted_iota(jnp.int32, (32, 256), 1) // 64
    for p in range(PARENTS):
        total = top_down[:, 64 * p:64 * p + 64]
        for j in range(0, 27, 4):
            tiles = []
            for i in range(j, min(j + 4, 27)):
                q = par_src_s[p, 0, i]
                d = lax.div(q, PARENTS)
                tiles.append(par_t[d >> 5, (d >> 4) & 1, (d >> 2) & 3, d & 3, q - d * PARENTS])
            weights = par_coup_v[p, j:j + len(tiles)].reshape(len(tiles) * 64, 64)
            total = total + dot(side_by_side(tiles)[:, :len(tiles) * 64], weights)
        field = leaf_acc[p] + dot_t(total.astype(BF16), lt_v[4 * p:4 * p + 4].reshape(256, 64))
        field = field.astype(BF16)
        spread = jnp.concatenate(
            [jnp.where(lane == c, field, jnp.zeros_like(field)) for c in range(4)], axis=0
        )
        far = dot(spread, basis_v[4 * p:4 * p + 4].reshape(256, 256))
        for c in range(4):
            g = 4 * p + c
            out_v[:, g * PTS:(g + 1) * PTS] = (near_acc[g] + far[32 * c:32 * c + 32]).astype(BF16)
    write = pltpu.make_async_copy(out_v, out, out_sem)
    write.start()

    for part in range(4):
        for stage in range(3):
            for k in range(3):
                hop(part, stage, k).wait_send()
        plane_relay(part).wait_send()
        for k in range(3):
            last_relay(part, k).wait_send()
    write.wait()


def local(
    right_sides, near_blocks, near_cols, near_count, basis, leaf_transfer, par_transfer,
    leaf_src, leaf_coup, par_src, par_coup, top_src, top_coup,
):
    vma = pltpu.VMEM
    call = pl.pallas_call(
        kernel,
        out_shape=jax.ShapeDtypeStruct((32, LEAVES * PTS), BF16),
        in_specs=[pl.BlockSpec(memory_space=pl.ANY)] * 13,
        out_specs=pl.BlockSpec(memory_space=pl.ANY),
        scratch_shapes=[
            vma((ZERO + 1, 32, PTS), BF16),
            vma((LEAVES, NEAR, PTS, PTS), BF16),
            vma((LEAVES, 64, PTS), BF16),
            vma((LEAVES, 64, 64), BF16),
            vma((PARENTS, 64, 64), BF16),
            vma((LEAVES, 8, 64, 64), BF16),
            vma((PARENTS, 27, 64, 64), BF16),
            vma((27, 64, 64), BF16),
            vma((32, LEAVES * PTS), BF16),
            pltpu.SMEM((NEAR, 1, LEAVES), jnp.int32),
            pltpu.SMEM((1, LEAVES), jnp.int32),
            pltpu.SMEM((8, LEAVES), jnp.int32),
            pltpu.SMEM((PARENTS, 1, 27), jnp.int32),
            pltpu.SMEM((1, 1, 27), jnp.int32),
            vma((LEAVES + 2 * HALO, 16, 128), BF16),
            vma((4, 2, 4, 4, PARENTS, 16, 128), BF16),
            vma((4, 2, 4, 4, 16, 128), BF16),
            vma((LEAVES, 32, PTS), F32),
            vma((PARENTS, 32, PTS), F32),
            pltpu.SemaphoreType.DMA((LEAVES,)),
            pltpu.SemaphoreType.DMA((12,)),
            pltpu.SemaphoreType.DMA((LEAVES,)),
            pltpu.SemaphoreType.DMA((4,)),
            pltpu.SemaphoreType.DMA((4,)),
            pltpu.SemaphoreType.DMA((36,)),
            pltpu.SemaphoreType.DMA((36,)),
            pltpu.SemaphoreType.DMA((16,)),
            pltpu.SemaphoreType.DMA((16,)),
            pltpu.SemaphoreType.DMA,
        ],
        compiler_params=pltpu.CompilerParams(
            collective_id=0, has_side_effects=True, vmem_limit_bytes=63 * 2**20
        ),
    )
    out = call(
        right_sides[:, 0],
        near_blocks[0],
        jnp.transpose(near_cols, (2, 0, 1)),
        near_count,
        jnp.swapaxes(basis[0], 1, 2),
        leaf_transfer[0],
        par_transfer[0],
        jnp.transpose(leaf_src[0], (1, 0)),
        leaf_coup[0],
        jnp.transpose(par_src, (1, 0, 2)),
        par_coup[0],
        top_src,
        top_coup[0, 0],
    )
    return out[:, None, :]


def solution(mesh):
    return jax.shard_map(
        local,
        mesh=mesh,
        in_specs=(
            P(None, "leaf", "clus"),
            P("leaf", "clus", None, None, None),
            P("leaf", "clus", None),
            P("leaf", "clus"),
            P("leaf", "clus", None, None),
            P("leaf", "clus", None, None),
            P("leaf", "clus", None, None),
            P("leaf", "clus", None),
            P("leaf", "clus", None, None, None),
            P("leaf", "clus", None),
            P("leaf", "clus", None, None, None),
            P("leaf", "clus", None),
            P("leaf", "clus", None, None, None),
        ),
        out_specs=P(None, "leaf", "clus"),
        check_vma=False,
    )
```

time: 138 us -> 38.8 us (0.28)
  blocking collectives: 43.4 us -> 0 us
  Pallas kernels: 0 us -> 36.9 us
  local copies, waits for them, and re-layouts: 37.7 us -> 1.77 us
  matrix products: 26.6 us -> 0 us
  between operations: 13.6 us -> 0.01 us
  starting transfers between devices: 11.7 us -> 0 us
  other arithmetic: 4.07 us -> 0 us
    all_gather x1 -> x0, blocking collectives: 43.4 us -> none  [local(): lax.all_gather(top_coeff.reshape(1, tile_size), ('clus', 'leaf'), axis=0,...]
    pallas_call x0 -> x1, Pallas kernels: none -> 36.9 us  [local(): call(right_sides[:, 0], near_blocks[0], jnp.transpose(near_cols, (2, 0, 1...]
    dot_general x9 -> x0, matrix products: 26.6 us -> none  [the longest x1 9.73 us: local(): jnp.einsum('rlnb,lnbc->rlc', picked, near_blocks[0], preferred_element_ty...]
    gather x4 -> x0, local copies, waits for them, and re-layouts: 13.3 us -> none  [the longest x2 8.12 us: local(): jnp.take(every_parent, source_device * parent_count + source_local, axis=0)]
    ppermute x4 -> x0, starting transfers between devices: 11.7 us -> none  [the longest x2 9.17 us: extended_2(): before = lax.ppermute(last, axis, up)]
    unnamed x27 -> x1, local copies, waits for them, and re-layouts: 9.98 us -> 1.77 us
    slice x4 -> x0, local copies, waits for them, and re-layouts: 4.52 us -> none  [the longest x3 2.95 us: extended_2(): last = lax.slice_in_dim(x, length - width, length, axis=dim)]
    concatenate x2 -> x0, local copies, waits for them, and re-layouts: 2.4 us -> none  [extended_2(): x = jnp.concatenate([before, x, after], axis=dim)]
  transfers between devices with their start and end apart: 5 -> 0, of which waited for: 0 -> 0; matrix products, arithmetic and copies ran while one was open for 26% -> 0% of each run, Pallas kernels for 0% -> 0%
where the time goes in v1:
time: 38.8 us; the launch traced here: 38.7 us
  Pallas kernels  36.9 us (95%)
  local copies, waits for them, and re-layouts  1.77 us (5%)
    pallas_call x1, Pallas kernels, local(): call(right_sides[:, 0], near_blocks[0], jnp.transpose(near_cols, (2, 0, 1...  36.9 us
    unnamed x1, local copies, waits for them, and re-layouts  1.77 us

profile of v1, /device:TPU:1, one launch (start us, length us, event | category | flops | bytes accessed | tf_op | source)
XLA Modules:
  0.0 38.7 jit_solution(4756097625257404164)
XLA Ops:
  0.0 36.9 %shard_map.127 = bf16[32,6144]{1,0:T(8,128)(2,1)} custom-call(bf16[32,6144]{1,0:T(8,128)(2,1)} %bitcast.22, bf16[24,5,256,256]{3,2,1,0:T(8,128)(2,1)} %bitcast.16, s32[5,1,24]{2,1,0:T(1,128)} %bitcast.27, s32[1,24]{1,0:T(1,128)} %count.1, bf16[24,64,256]{2,1,0:T(8,128)(2,1)} %bitcast.20, bf16[24,64,64]{2,1,0:T(8,128)(2,1)} %bitcast.23, ...), custom_call_target="tpu_custom_call" | custom-call | tf_op jit(solution)/shard_map/pallas_call | solution.py:343
  36.9 1.8 %copy.15 = bf16[32,1,6144]{2,0,1:T(8,128)(2,1)} copy(bf16[32,1,6144]{2,0,1:T(8,128)(2,1)} %bitcast.19) | data formatting | bytes 786432

commit v2 on v1

v2 whole, which is shorter than its diff:
```python
import jax
import jax.numpy as jnp
from jax import lax
from jax.experimental import pallas as pl
from jax.experimental.pallas import tpu as pltpu
from jax.sharding import PartitionSpec as P

F32 = jnp.float32
BF16 = jnp.bfloat16
LEAVES = 24
PARENTS = 6
HALO = 8
NEAR = 5
PTS = 256
ZERO = LEAVES + 2 * HALO
ORDERS = ("xyz", "yzx", "zxy")
ALL = (3, 0, 1, 2)
TOP = 3


def dot(a, b):
    return lax.dot_general(a, b, (((1,), (0,)), ((), ())), preferred_element_type=F32)


def dot_t(a, b):
    return lax.dot_general(a, b, (((1,), (1,)), ((), ())), preferred_element_type=F32)


def pack(y):
    return jnp.concatenate([y[:16], y[16:]], axis=1).astype(BF16)


def side_by_side(tiles):
    low = lax.broadcasted_iota(jnp.int32, (16, 128), 1) < 64
    columns = []
    for i in range(0, len(tiles), 2):
        a = tiles[i].astype(F32)
        b = tiles[i + 1].astype(F32) if i + 1 < len(tiles) else jnp.zeros_like(a)
        top = jnp.where(low, a, pltpu.roll(b, 64, 1))
        bottom = jnp.where(low, pltpu.roll(a, 64, 1), b)
        columns.append(jnp.concatenate([top, bottom], axis=0).astype(BF16))
    return jnp.concatenate(columns, axis=1)


def kernel(
    rhs, near, cols, count, basis, lt, pt, leaf_src, leaf_coup, par_src, par_coup, top_src, top_coup,
    out,
    x_own, x_v, near_v, basis_v, lt_v, pt_v, leaf_coup_v, par_coup_v, top_coup_v, out_v,
    cols_s, count_s, leaf_src_s, par_src_s, top_src_s,
    leaf_t, par_t, top_t, near_acc, leaf_acc,
    x_sem, in_sem, near_sem, halo_send, halo_recv, own_sem,
    spread_send, spread_recv, across_send, across_recv, onward_send, onward_recv,
    forward_send, forward_recv, share_send, share_recv, out_sem,
):
    clus = lax.axis_index("clus")
    tree = lax.axis_index("leaf")
    y, x = lax.div(clus, 4), lax.rem(clus, 4)
    z, core = lax.div(tree, 2), lax.rem(tree, 2)

    def device(dz=0, dc=0, dy=0, dx=0):
        return (
            lax.rem(y + dy, 4) * 4 + lax.rem(x + dx, 4),
            lax.rem(z + dz, 4) * 2 + lax.rem(core + dc, 2),
        )

    ta, tb, tc = x + core * (y - x), y + core * (z - y), z + core * (x - z)

    right, left = (lax.rem(clus + 1, 16), tree), (lax.rem(clus + 15, 16), tree)
    sibling = device(dc=1)
    along = {
        "z": [device(dz=d) for d in (1, 2, 3)],
        "y": [device(dy=d) for d in (1, 2, 3)],
        "x": [device(dx=d) for d in (1, 2, 3)],
    }
    partners = [right, left, sibling] + along["z"] + along["y"] + along["x"]
    barrier = pltpu.get_barrier_semaphore()
    for partner in partners:
        pl.semaphore_signal(barrier, inc=1, device_id=partner, device_id_type=pl.DeviceIdType.MESH)

    def fetch(i, src, dst):
        return pltpu.make_async_copy(src, dst, in_sem.at[i])

    def x_fetch(g):
        return pltpu.make_async_copy(rhs.at[:, pl.ds(g * PTS, PTS)], x_own.at[g], x_sem)

    for g in range(LEAVES):
        x_fetch(g).start()
    fetches = [
        fetch(1, basis, basis_v),
        fetch(2, lt, lt_v),
        fetch(3, pt, pt_v),
        fetch(4, cols, cols_s),
        fetch(5, count, count_s),
        fetch(6, leaf_src, leaf_src_s),
        fetch(7, par_src, par_src_s),
        fetch(8, top_src, top_src_s),
        fetch(9, leaf_coup, leaf_coup_v),
        fetch(10, par_coup, par_coup_v),
        fetch(11, top_coup, top_coup_v),
    ]
    for f in fetches[:3]:
        f.start()

    def near_fetch(i):
        pair = pl.ds(2 * i, 2)
        return pltpu.make_async_copy(near.at[pair], near_v.at[pair], near_sem.at[i])

    @pl.loop(0, LEAVES // 2)
    def _(i):
        near_fetch(i).start()

    for f in fetches[3:]:
        f.start()

    def remote(src, dst, send, recv, to):
        return pltpu.make_async_remote_copy(
            src_ref=src, dst_ref=dst, send_sem=send, recv_sem=recv, device_id=to,
            device_id_type=pl.DeviceIdType.MESH,
        )

    x_v[ZERO] = jnp.zeros((32, PTS), BF16)
    x_own[LEAVES] = jnp.zeros((32, PTS), BF16)
    pl.semaphore_wait(barrier, len(partners))
    def halo(i, own, table):
        lo, hi = pl.ds(0, HALO), pl.ds(LEAVES + HALO, HALO)
        return [
            remote(own.at[pl.ds(own.shape[0] - HALO, HALO)], table.at[lo], halo_send.at[i], halo_recv.at[i], right),
            remote(own.at[lo], table.at[hi], halo_send.at[i], halo_recv.at[i], left),
        ]

    def halo_wait(i, table):
        both = table.at[pl.ds(0, 2 * HALO)]
        remote(both, both, halo_send.at[i], halo_recv.at[i], right).wait()

    x_halos = halo(0, x_own.at[pl.ds(0, LEAVES)], x_v)
    leaf_halos = halo(1, leaf_t.at[pl.ds(HALO, LEAVES)], leaf_t)
    own = x_own.at[pl.ds(0, LEAVES)]
    pltpu.make_async_copy(own, own, x_sem).wait()
    for c in x_halos:
        c.start()
    own_copy = pltpu.make_async_copy(x_own.at[pl.ds(0, LEAVES)], x_v.at[pl.ds(HALO, LEAVES)], own_sem)
    own_copy.start()
    for f in fetches[:2]:
        f.wait()

    def unit(part):
        if part == TOP:
            return top_t.at[core, tc, tb, ta]
        return par_t.at[z, core, y, x, pl.ds(2 * part, 2)]

    def row(part, r, d):
        if part == TOP:
            return top_t.at[core, lax.rem(tc + 4 - d, 4), lax.rem(tb + 4 - r, 4)]
        a, b, c = ORDERS[part]
        at = {"z": z, "y": y, "x": x}
        at[b], at[c] = lax.rem(at[b] + 4 - r, 4), lax.rem(at[c] + 4 - d, 4)
        at[a] = slice(None)
        return par_t.at[at["z"], core, at["y"], at["x"], pl.ds(2 * part, 2)]

    def target(part, axis, d):
        if part == TOP:
            one, two = ("xyz"[axis], "yzx"[axis])
            return device(**{"d" + one: d * (1 - core), "d" + two: d * core})
        return along[ORDERS[part][axis]][d - 1]

    def kind(part):
        return int(part == TOP)

    def spread(part, k):
        i = kind(part)
        return remote(unit(part), unit(part), spread_send.at[i], spread_recv.at[i], target(part, 0, k + 1))

    def across(part, k):
        i = kind(part)
        ref = row(part, 0, 0)
        return remote(ref, ref, across_send.at[i], across_recv.at[i * 3 + k], target(part, 1, k + 1))

    def onward(part, r, way):
        i = kind(part)
        ref = row(part, r, 0)
        return remote(ref, ref, onward_send.at[i], onward_recv.at[i * 4 + r], target(part, 2, (1, 3)[way]))

    def forward(part, r):
        i = kind(part)
        d = 1 if r in (0, 3) else 3
        ref = row(part, r, d)
        return remote(ref, ref, forward_send.at[i], forward_recv.at[i * 4 + r], target(part, 2, d))

    def share(part, r, d):
        i = kind(part)
        ref = row(part, r, d)
        return remote(ref, ref, share_send.at[i], share_recv.at[i], sibling)

    def received(semaphore, ref):
        pltpu.make_async_copy(ref, ref, semaphore).wait()

    def rows(i, n):
        if i == 1:
            return top_t.at[core, 0, pl.ds(0, n)]
        return par_t.at[0, core, pl.ds(0, n)]

    for g in range(LEAVES):
        leaf_t[HALO + g] = pack(dot_t(x_own[g], basis_v[g]))
    for c in leaf_halos:
        c.start()
    parent_tiles = []
    for p in range(PARENTS):
        lhs = side_by_side([leaf_t[HALO + 4 * p + c] for c in range(4)])
        tile = pack(dot(lhs, lt_v[4 * p:4 * p + 4].reshape(256, 64)))
        parent_tiles.append(tile)
        par_t[z, core, y, x, p] = tile
        if p % 2:
            for k in (1, 0, 2):
                spread(p // 2, k).start()

    fetches[2].wait()
    lhs = side_by_side(parent_tiles)
    top_t[core, tc, tb, ta] = pack(dot(lhs, pt_v[...].reshape(PARENTS * 64, 64)))
    for k in (1, 0, 2):
        spread(TOP, k).start()

    first = clus * LEAVES - HALO

    def near_leaf(g, table, first, end):
        total = None
        for n in range(NEAR):
            live = jnp.clip(count_s[0, g] - n, 0, 1)
            at = end + live * (jnp.clip(cols_s[n, 0, g] - first, 0, end - 1) - end)
            term = dot(table[at], near_v[g, n])
            total = term if total is None else total + term
        near_acc[g] = total

    for f in fetches[3:8]:
        f.wait()

    def near_inner(lo, hi):
        @pl.loop(lo, hi)
        def _(i):
            near_fetch(i).wait()
            for g in (2 * i, 2 * i + 1):
                near_leaf(g, x_own, clus * LEAVES, LEAVES)

    def near_outer(lo, hi):
        @pl.loop(lo, hi)
        def _(i):
            near_fetch(i).wait()
            for g in (2 * i, 2 * i + 1):
                near_leaf(g, x_v, first, ZERO)

    near_inner(4, 6)
    received(spread_recv.at[0], par_t.at[0, core, 0, pl.ds(0, 3)])
    received(spread_recv.at[1], top_t.at[core, 0, 0, pl.ds(0, 3)])
    for part in ALL:
        for k in (0, 2, 1):
            across(part, k).start()
        for way in (0, 1):
            onward(part, 0, way).start()
        share(part, 0, 0).start()
    near_inner(6, 8)
    for r in (1, 3, 2):
        for i in (1, 0):
            received(across_recv.at[i * 3 + r - 1], rows(i, 1))
        for part in ALL:
            for way in (0, 1):
                onward(part, r, way).start()
            share(part, r, 0).start()
    own_copy.wait()
    halo_wait(0, x_v)
    for step, r in enumerate((0, 1, 3, 2)):
        lo = (8, 10, 0, 2)[step]
        near_outer(lo, lo + 2)
        for i in (1, 0):
            received(onward_recv.at[i * 4 + r], rows(i, 2))
        for part in ALL:
            forward(part, r).start()
            share(part, r, 1).start()
            share(part, r, 3).start()

    halo_wait(1, leaf_t)
    fetches[8].wait()

    @pl.loop(0, PARENTS)
    def _(p):
        fields = []
        for c in range(4):
            g = 4 * p + c
            total = None
            for half in range(2):
                tiles = []
                for j in range(4 * half, 4 * half + 4):
                    tiles.append(leaf_t[jnp.clip(leaf_src_s[j, g] - first, 0, ZERO - 1)])
                term = dot(side_by_side(tiles), leaf_coup_v[g, 4 * half:4 * half + 4].reshape(256, 64))
                total = term if total is None else total + term
            fields.append(total)
        leaf_acc[p] = jnp.concatenate(fields, axis=1)

    for r in (0, 1, 3, 2):
        for i in (1, 0):
            received(forward_recv.at[i * 4 + r], rows(i, 1))
        for part in ALL:
            share(part, r, 2).start()
    received(share_recv.at[1], top_t.at[0])
    received(share_recv.at[0], par_t.at[:, 0])

    fetches[10].wait()
    total = None
    for j in range(0, 27, 4):
        tiles = []
        for i in range(j, min(j + 4, 27)):
            t = top_src_s[0, 0, i]
            tz, tcore, ty, tx = t >> 5, (t >> 4) & 1, (t >> 2) & 3, t & 3
            tiles.append(top_t[tcore, tz + tcore * (tx - tz), ty + tcore * (tz - ty), tx + tcore * (ty - tx)])
        weights = top_coup_v[j:j + len(tiles)].reshape(len(tiles) * 64, 64)
        term = dot(side_by_side(tiles)[:, :len(tiles) * 64], weights)
        total = term if total is None else total + term
    top_field = total.astype(BF16)
    all_parents = par_t.reshape(768, 16, 128)
    top_down = dot_t(top_field, pt_v[...].reshape(PARENTS * 64, 64))
    fetches[9].wait()
    lane = lax.broadcasted_iota(jnp.int32, (32, 256), 1) // 64
    for p in range(PARENTS):
        total = top_down[:, 64 * p:64 * p + 64]
        for j in range(0, 27, 4):
            tiles = []
            for i in range(j, min(j + 4, 27)):
                q = par_src_s[p, 0, i]
                tiles.append(all_parents[q])
            weights = par_coup_v[p, j:j + len(tiles)].reshape(len(tiles) * 64, 64)
            total = total + dot(side_by_side(tiles)[:, :len(tiles) * 64], weights)
        field = leaf_acc[p] + dot_t(total.astype(BF16), lt_v[4 * p:4 * p + 4].reshape(256, 64))
        field = field.astype(BF16)
        masked = jnp.concatenate(
            [jnp.where(lane == c, field, jnp.zeros_like(field)) for c in range(4)], axis=0
        )
        far = dot(masked, basis_v[4 * p:4 * p + 4].reshape(256, 256))
        for c in range(4):
            g = 4 * p + c
            out_v[:, g * PTS:(g + 1) * PTS] = (near_acc[g] + far[32 * c:32 * c + 32]).astype(BF16)
        columns = pl.ds(4 * p * PTS, 4 * PTS)
        pltpu.make_async_copy(out_v.at[:, columns], out.at[:, columns], out_sem).start()

    for i, table in enumerate((par_t.at[:, core], top_t.at[core])):
        pieces = par_t.at[0, core, 0, pl.ds(0, 3)] if i == 0 else top_t.at[core, 0, 0, pl.ds(0, 3)]
        received(spread_send.at[i], pieces)
        received(across_send.at[i], rows(i, 3))
        received(onward_send.at[i], par_t.at[pl.ds(0, 2), core] if i == 0 else top_t.at[core, pl.ds(0, 2)])
        received(forward_send.at[i], rows(i, 4))
        received(share_send.at[i], table)
    received(out_sem, out_v)


def local(
    right_sides, near_blocks, near_cols, near_count, basis, leaf_transfer, par_transfer,
    leaf_src, leaf_coup, par_src, par_coup, top_src, top_coup,
):
    vma = pltpu.VMEM
    call = pl.pallas_call(
        kernel,
        out_shape=jax.ShapeDtypeStruct((32, LEAVES * PTS), BF16),
        in_specs=[pl.BlockSpec(memory_space=pl.ANY)] * 13,
        out_specs=pl.BlockSpec(memory_space=pl.ANY),
        scratch_shapes=[
            vma((LEAVES + 1, 32, PTS), BF16),
            vma((ZERO + 1, 32, PTS), BF16),
            vma((LEAVES, NEAR, PTS, PTS), BF16),
            vma((LEAVES, 64, PTS), BF16),
            vma((LEAVES, 64, 64), BF16),
            vma((PARENTS, 64, 64), BF16),
            vma((LEAVES, 8, 64, 64), BF16),
            vma((PARENTS, 27, 64, 64), BF16),
            vma((27, 64, 64), BF16),
            vma((32, LEAVES * PTS), BF16),
            pltpu.SMEM((NEAR, 1, LEAVES), jnp.int32),
            pltpu.SMEM((1, LEAVES), jnp.int32),
            pltpu.SMEM((8, LEAVES), jnp.int32),
            pltpu.SMEM((PARENTS, 1, 27), jnp.int32),
            pltpu.SMEM((1, 1, 27), jnp.int32),
            vma((LEAVES + 2 * HALO, 16, 128), BF16),
            vma((4, 2, 4, 4, PARENTS, 16, 128), BF16),
            vma((2, 4, 4, 4, 16, 128), BF16),
            vma((LEAVES, 32, PTS), F32),
            vma((PARENTS, 32, PTS), F32),
            pltpu.SemaphoreType.DMA,
            pltpu.SemaphoreType.DMA((12,)),
            pltpu.SemaphoreType.DMA((LEAVES // 2,)),
            pltpu.SemaphoreType.DMA((2,)),
            pltpu.SemaphoreType.DMA((2,)),
            pltpu.SemaphoreType.DMA,
            pltpu.SemaphoreType.DMA((2,)),
            pltpu.SemaphoreType.DMA((2,)),
            pltpu.SemaphoreType.DMA((2,)),
            pltpu.SemaphoreType.DMA((6,)),
            pltpu.SemaphoreType.DMA((2,)),
            pltpu.SemaphoreType.DMA((8,)),
            pltpu.SemaphoreType.DMA((2,)),
            pltpu.SemaphoreType.DMA((8,)),
            pltpu.SemaphoreType.DMA((2,)),
            pltpu.SemaphoreType.DMA((2,)),
            pltpu.SemaphoreType.DMA,
        ],
        compiler_params=pltpu.CompilerParams(
            collective_id=0, has_side_effects=True, vmem_limit_bytes=63 * 2**20
        ),
    )
    out = call(
        right_sides[:, 0],
        near_blocks[0],
        jnp.transpose(near_cols, (2, 0, 1)),
        near_count,
        jnp.swapaxes(basis[0], 1, 2),
        leaf_transfer[0],
        par_transfer[0],
        jnp.transpose(leaf_src[0], (1, 0)),
        leaf_coup[0],
        jnp.transpose(par_src, (1, 0, 2)),
        par_coup[0],
        top_src,
        top_coup[0, 0],
    )
    return out[:, None, :]


def solution(mesh):
    return jax.shard_map(
        local,
        mesh=mesh,
        in_specs=(
            P(None, "leaf", "clus"),
            P("leaf", "clus", None, None, None),
            P("leaf", "clus", None),
            P("leaf", "clus"),
            P("leaf", "clus", None, None),
            P("leaf", "clus", None, None),
            P("leaf", "clus", None, None),
            P("leaf", "clus", None),
            P("leaf", "clus", None, None, None),
            P("leaf", "clus", None),
            P("leaf", "clus", None, None, None),
            P("leaf", "clus", None),
            P("leaf", "clus", None, None, None),
        ),
        out_specs=P(None, "leaf", "clus"),
        check_vma=False,
    )
```

time: 38.8 us -> 35.1 us (0.905)
  Pallas kernels: 36.9 us -> 33.2 us
    pallas_call x1, Pallas kernels: 36.9 us -> 33.2 us  [local(): call(right_sides[:, 0], near_blocks[0], jnp.transpose(near_cols, (2, 0, 1...]
where the time goes in v2:
time: 35.1 us; the launch traced here: 35 us
  Pallas kernels  33.2 us (95%)
  local copies, waits for them, and re-layouts  1.77 us (5%)
    pallas_call x1, Pallas kernels, local(): call(right_sides[:, 0], near_blocks[0], jnp.transpose(near_cols, (2, 0, 1...  33.2 us
    unnamed x1, local copies, waits for them, and re-layouts  1.77 us

profile of v2, /device:TPU:1, one launch (start us, length us, event | category | flops | bytes accessed | tf_op | source)
XLA Modules:
  0.0 35.0 jit_solution(9657614652529813470)
XLA Ops:
  0.0 33.2 %shard_map.127 = bf16[32,6144]{1,0:T(8,128)(2,1)} custom-call(bf16[32,6144]{1,0:T(8,128)(2,1)} %bitcast.22, bf16[24,5,256,256]{3,2,1,0:T(8,128)(2,1)} %bitcast.16, s32[5,1,24]{2,1,0:T(1,128)} %bitcast.27, s32[1,24]{1,0:T(1,128)} %count.1, bf16[24,64,256]{2,1,0:T(8,128)(2,1)} %bitcast.20, bf16[24,64,64]{2,1,0:T(8,128)(2,1)} %bitcast.23, ...), custom_call_target="tpu_custom_call" | custom-call | tf_op jit(solution)/shard_map/pallas_call | solution.py:405
  33.2 1.8 %copy.15 = bf16[32,1,6144]{2,0,1:T(8,128)(2,1)} copy(bf16[32,1,6144]{2,0,1:T(8,128)(2,1)} %bitcast.19) | data formatting | bytes 786432

commit v3 on v2

--- a/solution.py
+++ b/solution.py
@@ -15,6 +15,7 @@
 ZERO = LEAVES + 2 * HALO
 ORDERS = ("xyz", "yzx", "zxy")
 ALL = (3, 0, 1, 2)
+QUADS = 7
 TOP = 3
 
 
@@ -47,10 +48,10 @@
     out,
     x_own, x_v, near_v, basis_v, lt_v, pt_v, leaf_coup_v, par_coup_v, top_coup_v, out_v,
     cols_s, count_s, leaf_src_s, par_src_s, top_src_s,
-    leaf_t, par_t, top_t, near_acc, leaf_acc,
+    leaf_t, par_t, top_t, par_w, near_acc, leaf_acc,
     x_sem, in_sem, near_sem, halo_send, halo_recv, own_sem,
     spread_send, spread_recv, across_send, across_recv, onward_send, onward_recv,
-    forward_send, forward_recv, share_send, share_recv, out_sem,
+    opposite_send, opposite_recv, share_send, share_recv, out_sem,
 ):
     clus = lax.axis_index("clus")
     tree = lax.axis_index("leaf")
@@ -94,8 +95,8 @@
         fetch(6, leaf_src, leaf_src_s),
         fetch(7, par_src, par_src_s),
         fetch(8, top_src, top_src_s),
-        fetch(9, leaf_coup, leaf_coup_v),
-        fetch(10, par_coup, par_coup_v),
+        fetch(9, par_coup, par_coup_v),
+        fetch(10, leaf_coup, leaf_coup_v),
         fetch(11, top_coup, top_coup_v),
     ]
     for f in fetches[:3]:
@@ -105,12 +106,20 @@
         pair = pl.ds(2 * i, 2)
         return pltpu.make_async_copy(near.at[pair], near_v.at[pair], near_sem.at[i])
 
-    @pl.loop(0, LEAVES // 2)
-    def _(i):
-        near_fetch(i).start()
-
-    for f in fetches[3:]:
+    for f in fetches[3:8]:
         f.start()
+
+    def near_fetches(lo, hi):
+        @pl.loop(lo, hi)
+        def _(i):
+            near_fetch(i).start()
+
+    near_fetches(4, 8)
+    for f in fetches[8:]:
+        f.start()
+    near_fetches(8, 12)
+    near_fetches(0, 4)
+
 
     def remote(src, dst, send, recv, to):
         return pltpu.make_async_remote_copy(
@@ -120,24 +129,24 @@
 
     x_v[ZERO] = jnp.zeros((32, PTS), BF16)
     x_own[LEAVES] = jnp.zeros((32, PTS), BF16)
-    pl.semaphore_wait(barrier, len(partners))
-    def halo(i, own, table):
-        lo, hi = pl.ds(0, HALO), pl.ds(LEAVES + HALO, HALO)
-        return [
-            remote(own.at[pl.ds(own.shape[0] - HALO, HALO)], table.at[lo], halo_send.at[i], halo_recv.at[i], right),
-            remote(own.at[lo], table.at[hi], halo_send.at[i], halo_recv.at[i], left),
-        ]
+    def leaf_columns(g):
+        return rhs.at[:, pl.ds(g * PTS, PTS)]
+
+    x_halos = [
+        remote(x_own.at[pl.ds(LEAVES - HALO, HALO)], x_v.at[pl.ds(0, HALO)], halo_send.at[0], halo_recv.at[0], right),
+        remote(x_own.at[pl.ds(0, HALO)], x_v.at[pl.ds(LEAVES + HALO, HALO)], halo_send.at[0], halo_recv.at[0], left),
+    ]
+    leaf_halos = [
+        remote(leaf_t.at[pl.ds(LEAVES, HALO)], leaf_t.at[pl.ds(0, HALO)], halo_send.at[1], halo_recv.at[1], right),
+        remote(leaf_t.at[pl.ds(HALO, HALO)], leaf_t.at[pl.ds(LEAVES + HALO, HALO)], halo_send.at[1], halo_recv.at[1], left),
+    ]
 
     def halo_wait(i, table):
         both = table.at[pl.ds(0, 2 * HALO)]
         remote(both, both, halo_send.at[i], halo_recv.at[i], right).wait()
 
-    x_halos = halo(0, x_own.at[pl.ds(0, LEAVES)], x_v)
-    leaf_halos = halo(1, leaf_t.at[pl.ds(HALO, LEAVES)], leaf_t)
     own = x_own.at[pl.ds(0, LEAVES)]
     pltpu.make_async_copy(own, own, x_sem).wait()
-    for c in x_halos:
-        c.start()
     own_copy = pltpu.make_async_copy(x_own.at[pl.ds(0, LEAVES)], x_v.at[pl.ds(HALO, LEAVES)], own_sem)
     own_copy.start()
     for f in fetches[:2]:
@@ -163,44 +172,34 @@
             return device(**{"d" + one: d * (1 - core), "d" + two: d * core})
         return along[ORDERS[part][axis]][d - 1]
 
-    def kind(part):
-        return int(part == TOP)
-
     def spread(part, k):
-        i = kind(part)
-        return remote(unit(part), unit(part), spread_send.at[i], spread_recv.at[i], target(part, 0, k + 1))
+        return remote(unit(part), unit(part), spread_send, spread_recv, target(part, 0, k + 1))
 
     def across(part, k):
-        i = kind(part)
         ref = row(part, 0, 0)
-        return remote(ref, ref, across_send.at[i], across_recv.at[i * 3 + k], target(part, 1, k + 1))
+        return remote(ref, ref, across_send, across_recv.at[k], target(part, 1, k + 1))
 
     def onward(part, r, way):
-        i = kind(part)
         ref = row(part, r, 0)
-        return remote(ref, ref, onward_send.at[i], onward_recv.at[i * 4 + r], target(part, 2, (1, 3)[way]))
-
-    def forward(part, r):
-        i = kind(part)
-        d = 1 if r in (0, 3) else 3
+        return remote(ref, ref, onward_send, onward_recv.at[r], target(part, 2, (1, 3)[way]))
+
+    def opposite(part, r):
+        ref = row(part, r, 0)
+        return remote(ref, ref, opposite_send, opposite_recv.at[r], target(part, 2, 2))
+
+    def share(part, r, d):
         ref = row(part, r, d)
-        return remote(ref, ref, forward_send.at[i], forward_recv.at[i * 4 + r], target(part, 2, d))
-
-    def share(part, r, d):
-        i = kind(part)
-        ref = row(part, r, d)
-        return remote(ref, ref, share_send.at[i], share_recv.at[i], sibling)
-
-    def received(semaphore, ref):
+        return remote(ref, ref, share_send, share_recv.at[int(part == TOP)], sibling)
+
+    all_parents = par_t.reshape(768, 16, 128)
+
+    def await_tiles(semaphore, n):
+        ref = all_parents.at[pl.ds(0, n)]
         pltpu.make_async_copy(ref, ref, semaphore).wait()
-
-    def rows(i, n):
-        if i == 1:
-            return top_t.at[core, 0, pl.ds(0, n)]
-        return par_t.at[0, core, pl.ds(0, n)]
 
     for g in range(LEAVES):
         leaf_t[HALO + g] = pack(dot_t(x_own[g], basis_v[g]))
+    pl.semaphore_wait(barrier, len(partners))
     for c in leaf_halos:
         c.start()
     parent_tiles = []
@@ -218,6 +217,15 @@
     top_t[core, tc, tb, ta] = pack(dot(lhs, pt_v[...].reshape(PARENTS * 64, 64)))
     for k in (1, 0, 2):
         spread(TOP, k).start()
+    for c in x_halos:
+        c.start()
+
+    def pack_weights(q, present):
+        nothing = jnp.zeros((64, 64), BF16)
+        for h in range(2):
+            for k in range(4):
+                blocks = [par_coup_v[3 * h + n, 4 * q + k] if k < present else nothing for n in range(3)]
+                par_w[h, q, 64 * k:64 * k + 64] = jnp.concatenate(blocks + [nothing], axis=1)
 
     first = clus * LEAVES - HALO
 
@@ -247,37 +255,24 @@
             for g in (2 * i, 2 * i + 1):
                 near_leaf(g, x_v, first, ZERO)
 
-    near_inner(4, 6)
-    received(spread_recv.at[0], par_t.at[0, core, 0, pl.ds(0, 3)])
-    received(spread_recv.at[1], top_t.at[core, 0, 0, pl.ds(0, 3)])
+    near_inner(4, 8)
+    await_tiles(spread_recv, 3 * 7)
     for part in ALL:
         for k in (0, 2, 1):
             across(part, k).start()
         for way in (0, 1):
             onward(part, 0, way).start()
+        opposite(part, 0).start()
         share(part, 0, 0).start()
-    near_inner(6, 8)
-    for r in (1, 3, 2):
-        for i in (1, 0):
-            received(across_recv.at[i * 3 + r - 1], rows(i, 1))
-        for part in ALL:
-            for way in (0, 1):
-                onward(part, r, way).start()
-            share(part, r, 0).start()
-    own_copy.wait()
-    halo_wait(0, x_v)
-    for step, r in enumerate((0, 1, 3, 2)):
-        lo = (8, 10, 0, 2)[step]
-        near_outer(lo, lo + 2)
-        for i in (1, 0):
-            received(onward_recv.at[i * 4 + r], rows(i, 2))
-        for part in ALL:
-            forward(part, r).start()
-            share(part, r, 1).start()
-            share(part, r, 3).start()
-
+    fetches[8].wait()
+
+    @pl.loop(0, QUADS - 1)
+    def _(q):
+        pack_weights(q, 4)
+
+    pack_weights(QUADS - 1, 3)
     halo_wait(1, leaf_t)
-    fetches[8].wait()
+    fetches[9].wait()
 
     @pl.loop(0, PARENTS)
     def _(p):
@@ -294,13 +289,32 @@
             fields.append(total)
         leaf_acc[p] = jnp.concatenate(fields, axis=1)
 
+    for r in (1, 3, 2):
+        await_tiles(across_recv.at[r - 1], 4 * 7)
+        for part in ALL:
+            for way in (0, 1):
+                onward(part, r, way).start()
+            opposite(part, r).start()
+            share(part, r, 0).start()
+    own_copy.wait()
+    halo_wait(0, x_v)
+    near_outer(8, 10)
     for r in (0, 1, 3, 2):
-        for i in (1, 0):
-            received(forward_recv.at[i * 4 + r], rows(i, 1))
+        await_tiles(onward_recv.at[r], 8 * 7)
+        for part in ALL:
+            share(part, r, 1).start()
+            share(part, r, 3).start()
+        if r == 0:
+            near_outer(10, 12)
+        if r == 1:
+            near_outer(0, 2)
+        if r == 3:
+            near_outer(2, 4)
+        await_tiles(opposite_recv.at[r], 4 * 7)
         for part in ALL:
             share(part, r, 2).start()
-    received(share_recv.at[1], top_t.at[0])
-    received(share_recv.at[0], par_t.at[:, 0])
+
+    await_tiles(share_recv.at[1], 64)
 
     fetches[10].wait()
     total = None
@@ -314,19 +328,21 @@
         term = dot(side_by_side(tiles)[:, :len(tiles) * 64], weights)
         total = term if total is None else total + term
     top_field = total.astype(BF16)
-    all_parents = par_t.reshape(768, 16, 128)
+    await_tiles(share_recv.at[0], 384)
     top_down = dot_t(top_field, pt_v[...].reshape(PARENTS * 64, 64))
-    fetches[9].wait()
     lane = lax.broadcasted_iota(jnp.int32, (32, 256), 1) // 64
+    sums = []
+    for h in range(2):
+        total = None
+        for q in range(QUADS):
+            lhs = []
+            for p in range(3 * h, 3 * h + 3):
+                lhs.append(side_by_side([all_parents[par_src_s[p, 0, i]] for i in range(4 * q, min(4 * q + 4, 27))]))
+            term = dot(jnp.concatenate(lhs, axis=0), par_w[h, q])
+            total = term if total is None else total + term
+        sums += [total[32 * n:32 * n + 32, 64 * n:64 * n + 64] for n in range(3)]
     for p in range(PARENTS):
-        total = top_down[:, 64 * p:64 * p + 64]
-        for j in range(0, 27, 4):
-            tiles = []
-            for i in range(j, min(j + 4, 27)):
-                q = par_src_s[p, 0, i]
-                tiles.append(all_parents[q])
-            weights = par_coup_v[p, j:j + len(tiles)].reshape(len(tiles) * 64, 64)
-            total = total + dot(side_by_side(tiles)[:, :len(tiles) * 64], weights)
+        total = sums[p] + top_down[:, 64 * p:64 * p + 64]
         field = leaf_acc[p] + dot_t(total.astype(BF16), lt_v[4 * p:4 * p + 4].reshape(256, 64))
         field = field.astype(BF16)
         masked = jnp.concatenate(
@@ -339,14 +355,12 @@
         columns = pl.ds(4 * p * PTS, 4 * PTS)
         pltpu.make_async_copy(out_v.at[:, columns], out.at[:, columns], out_sem).start()
 
-    for i, table in enumerate((par_t.at[:, core], top_t.at[core])):
-        pieces = par_t.at[0, core, 0, pl.ds(0, 3)] if i == 0 else top_t.at[core, 0, 0, pl.ds(0, 3)]
-        received(spread_send.at[i], pieces)
-        received(across_send.at[i], rows(i, 3))
-        received(onward_send.at[i], par_t.at[pl.ds(0, 2), core] if i == 0 else top_t.at[core, pl.ds(0, 2)])
-        received(forward_send.at[i], rows(i, 4))
-        received(share_send.at[i], table)
-    received(out_sem, out_v)
+    await_tiles(spread_send, 3 * 7)
+    await_tiles(across_send, 12 * 7)
+    await_tiles(onward_send, 32 * 7)
+    await_tiles(opposite_send, 16 * 7)
+    await_tiles(share_send, 64 * 7)
+    pltpu.make_async_copy(out_v, out_v, out_sem).wait()
 
 
 def local(
@@ -378,6 +392,7 @@
             vma((LEAVES + 2 * HALO, 16, 128), BF16),
             vma((4, 2, 4, 4, PARENTS, 16, 128), BF16),
             vma((2, 4, 4, 4, 16, 128), BF16),
+            vma((2, QUADS, 256, 256), BF16),
             vma((LEAVES, 32, PTS), F32),
             vma((PARENTS, 32, PTS), F32),
             pltpu.SemaphoreType.DMA,
@@ -386,15 +401,15 @@
             pltpu.SemaphoreType.DMA((2,)),
             pltpu.SemaphoreType.DMA((2,)),
             pltpu.SemaphoreType.DMA,
-            pltpu.SemaphoreType.DMA((2,)),
-            pltpu.SemaphoreType.DMA((2,)),
-            pltpu.SemaphoreType.DMA((2,)),
-            pltpu.SemaphoreType.DMA((6,)),
-            pltpu.SemaphoreType.DMA((2,)),
-            pltpu.SemaphoreType.DMA((8,)),
-            pltpu.SemaphoreType.DMA((2,)),
-            pltpu.SemaphoreType.DMA((8,)),
-            pltpu.SemaphoreType.DMA((2,)),
+            pltpu.SemaphoreType.DMA,
+            pltpu.SemaphoreType.DMA,
+            pltpu.SemaphoreType.DMA,
+            pltpu.SemaphoreType.DMA((3,)),
+            pltpu.SemaphoreType.DMA,
+            pltpu.SemaphoreType.DMA((4,)),
+            pltpu.SemaphoreType.DMA,
+            pltpu.SemaphoreType.DMA((4,)),
+            pltpu.SemaphoreType.DMA,
             pltpu.SemaphoreType.DMA((2,)),
             pltpu.SemaphoreType.DMA,
         ],

time: 35.1 us -> 29.5 us (0.84)
  Pallas kernels: 33.2 us -> 27.6 us
    pallas_call x1, Pallas kernels: 33.2 us -> 27.6 us  [local(): call(right_sides[:, 0], near_blocks[0], jnp.transpose(near_cols, (2, 0, 1...]
where the time goes in v3:
time: 29.5 us; the launch traced here: 29.4 us
  Pallas kernels  27.6 us (94%)
  local copies, waits for them, and re-layouts  1.77 us (6%)
    pallas_call x1, Pallas kernels, local(): call(right_sides[:, 0], near_blocks[0], jnp.transpose(near_cols, (2, 0, 1...  27.6 us
    unnamed x1, local copies, waits for them, and re-layouts  1.77 us

profile of v3, /device:TPU:1, one launch (start us, length us, event | category | flops | bytes accessed | tf_op | source)
XLA Modules:
  0.0 29.4 jit_solution(9990610508958441469)
XLA Ops:
  0.0 27.6 %shard_map.127 = bf16[32,6144]{1,0:T(8,128)(2,1)} custom-call(bf16[32,6144]{1,0:T(8,128)(2,1)} %bitcast.22, bf16[24,5,256,256]{3,2,1,0:T(8,128)(2,1)} %bitcast.16, s32[5,1,24]{2,1,0:T(1,128)} %bitcast.27, s32[1,24]{1,0:T(1,128)} %count.1, bf16[24,64,256]{2,1,0:T(8,128)(2,1)} %bitcast.20, bf16[24,64,64]{2,1,0:T(8,128)(2,1)} %bitcast.23, ...), custom_call_target="tpu_custom_call" | custom-call | tf_op jit(solution)/shard_map/pallas_call | solution.py:420
  27.6 1.8 %copy.15 = bf16[32,1,6144]{2,0,1:T(8,128)(2,1)} copy(bf16[32,1,6144]{2,0,1:T(8,128)(2,1)} %bitcast.19) | data formatting | bytes 786432

commit v4 on v3

--- a/solution.py
+++ b/solution.py
@@ -15,6 +15,7 @@
 ZERO = LEAVES + 2 * HALO
 ORDERS = ("xyz", "yzx", "zxy")
 ALL = (3, 0, 1, 2)
+TILES = (2, 2, 2, 1)
 QUADS = 7
 TOP = 3
 
@@ -129,8 +130,6 @@
 
     x_v[ZERO] = jnp.zeros((32, PTS), BF16)
     x_own[LEAVES] = jnp.zeros((32, PTS), BF16)
-    def leaf_columns(g):
-        return rhs.at[:, pl.ds(g * PTS, PTS)]
 
     x_halos = [
         remote(x_own.at[pl.ds(LEAVES - HALO, HALO)], x_v.at[pl.ds(0, HALO)], halo_send.at[0], halo_recv.at[0], right),
@@ -173,11 +172,11 @@
         return along[ORDERS[part][axis]][d - 1]
 
     def spread(part, k):
-        return remote(unit(part), unit(part), spread_send, spread_recv, target(part, 0, k + 1))
+        return remote(unit(part), unit(part), spread_send, spread_recv.at[part], target(part, 0, k + 1))
 
     def across(part, k):
         ref = row(part, 0, 0)
-        return remote(ref, ref, across_send, across_recv.at[k], target(part, 1, k + 1))
+        return remote(ref, ref, across_send, across_recv.at[4 * k + part], target(part, 1, k + 1))
 
     def onward(part, r, way):
         ref = row(part, r, 0)
@@ -256,8 +255,8 @@
                 near_leaf(g, x_v, first, ZERO)
 
     near_inner(4, 8)
-    await_tiles(spread_recv, 3 * 7)
     for part in ALL:
+        await_tiles(spread_recv.at[part], 3 * TILES[part])
         for k in (0, 2, 1):
             across(part, k).start()
         for way in (0, 1):
@@ -289,9 +288,9 @@
             fields.append(total)
         leaf_acc[p] = jnp.concatenate(fields, axis=1)
 
-    for r in (1, 3, 2):
-        await_tiles(across_recv.at[r - 1], 4 * 7)
+    for r in (3, 1, 2):
         for part in ALL:
+            await_tiles(across_recv.at[4 * (r - 1) + part], 4 * TILES[part])
             for way in (0, 1):
                 onward(part, r, way).start()
             opposite(part, r).start()
@@ -299,16 +298,16 @@
     own_copy.wait()
     halo_wait(0, x_v)
     near_outer(8, 10)
-    for r in (0, 1, 3, 2):
+    for r in (0, 3, 1, 2):
         await_tiles(onward_recv.at[r], 8 * 7)
         for part in ALL:
             share(part, r, 1).start()
             share(part, r, 3).start()
         if r == 0:
             near_outer(10, 12)
+        if r == 3:
+            near_outer(0, 2)
         if r == 1:
-            near_outer(0, 2)
-        if r == 3:
             near_outer(2, 4)
         await_tiles(opposite_recv.at[r], 4 * 7)
         for part in ALL:
@@ -402,9 +401,9 @@
             pltpu.SemaphoreType.DMA((2,)),
             pltpu.SemaphoreType.DMA,
             pltpu.SemaphoreType.DMA,
-            pltpu.SemaphoreType.DMA,
-            pltpu.SemaphoreType.DMA,
-            pltpu.SemaphoreType.DMA((3,)),
+            pltpu.SemaphoreType.DMA((4,)),
+            pltpu.SemaphoreType.DMA,
+            pltpu.SemaphoreType.DMA((12,)),
             pltpu.SemaphoreType.DMA,
             pltpu.SemaphoreType.DMA((4,)),
             pltpu.SemaphoreType.DMA,

time: 29.5 us -> 28.9 us (0.980)
  Pallas kernels: 27.6 us -> 27 us
    pallas_call x1, Pallas kernels: 27.6 us -> 27 us  [local(): call(right_sides[:, 0], near_blocks[0], jnp.transpose(near_cols, (2, 0, 1...]
where the time goes in v4:
time: 28.9 us; the launch traced here: 28.8 us
  Pallas kernels  27 us (93%)
  local copies, waits for them, and re-layouts  1.77 us (6%)
    pallas_call x1, Pallas kernels, local(): call(right_sides[:, 0], near_blocks[0], jnp.transpose(near_cols, (2, 0, 1...  27 us
    unnamed x1, local copies, waits for them, and re-layouts  1.77 us

profile of v4, /device:TPU:1, one launch (start us, length us, event | category | flops | bytes accessed | tf_op | source)
XLA Modules:
  0.0 28.8 jit_solution(16759729495253908470)
XLA Ops:
  0.0 27.0 %shard_map.127 = bf16[32,6144]{1,0:T(8,128)(2,1)} custom-call(bf16[32,6144]{1,0:T(8,128)(2,1)} %bitcast.22, bf16[24,5,256,256]{3,2,1,0:T(8,128)(2,1)} %bitcast.16, s32[5,1,24]{2,1,0:T(1,128)} %bitcast.27, s32[1,24]{1,0:T(1,128)} %count.1, bf16[24,64,256]{2,1,0:T(8,128)(2,1)} %bitcast.20, bf16[24,64,64]{2,1,0:T(8,128)(2,1)} %bitcast.23, ...), custom_call_target="tpu_custom_call" | custom-call | tf_op jit(solution)/shard_map/pallas_call | solution.py:419
  27.0 1.8 %copy.15 = bf16[32,1,6144]{2,0,1:T(8,128)(2,1)} copy(bf16[32,1,6144]{2,0,1:T(8,128)(2,1)} %bitcast.19) | data formatting | bytes 786432

commit v5 on v4

--- a/solution.py
+++ b/solution.py
@@ -254,7 +254,7 @@
             for g in (2 * i, 2 * i + 1):
                 near_leaf(g, x_v, first, ZERO)
 
-    near_inner(4, 8)
+    near_inner(4, 6)
     for part in ALL:
         await_tiles(spread_recv.at[part], 3 * TILES[part])
         for k in (0, 2, 1):
@@ -263,6 +263,7 @@
             onward(part, 0, way).start()
         opposite(part, 0).start()
         share(part, 0, 0).start()
+    near_inner(6, 8)
     fetches[8].wait()
 
     @pl.loop(0, QUADS - 1)

time: 28.9 us -> 28.9 us (level)
  no operation moved by 1% of the time
where the time goes in v5:
time: 28.9 us; the launch traced here: 28.6 us
  Pallas kernels  26.8 us (93%)
  local copies, waits for them, and re-layouts  1.77 us (6%)
    pallas_call x1, Pallas kernels, local(): call(right_sides[:, 0], near_blocks[0], jnp.transpose(near_cols, (2, 0, 1...  26.8 us
    unnamed x1, local copies, waits for them, and re-layouts  1.77 us

profile of v5, /device:TPU:1, one launch (start us, length us, event | category | flops | bytes accessed | tf_op | source)
XLA Modules:
  0.0 28.6 jit_solution(11242262623014400364)
XLA Ops:
  0.0 26.8 %shard_map.127 = bf16[32,6144]{1,0:T(8,128)(2,1)} custom-call(bf16[32,6144]{1,0:T(8,128)(2,1)} %bitcast.22, bf16[24,5,256,256]{3,2,1,0:T(8,128)(2,1)} %bitcast.16, s32[5,1,24]{2,1,0:T(1,128)} %bitcast.27, s32[1,24]{1,0:T(1,128)} %count.1, bf16[24,64,256]{2,1,0:T(8,128)(2,1)} %bitcast.20, bf16[24,64,64]{2,1,0:T(8,128)(2,1)} %bitcast.23, ...), custom_call_target="tpu_custom_call" | custom-call | tf_op jit(solution)/shard_map/pallas_call | solution.py:420
  26.8 1.8 %copy.15 = bf16[32,1,6144]{2,0,1:T(8,128)(2,1)} copy(bf16[32,1,6144]{2,0,1:T(8,128)(2,1)} %bitcast.19) | data formatting | bytes 786432
